TPU v7x, 32 devices: a whole 2x2x4 slice. The times are simulated.
32 devices in a mesh: grp: 2 (over y), dp: 16 (over z, x, core).
Axes of the slice: x: 2, y: 2, z: 4, core: 2. Of those that a mesh axis runs over, the one named last changes fastest.
Arguments:
- acts: bfloat16 [16384, 2560], P(('grp', 'dp')), may hold values from -18 to 18
- cotangents: bfloat16 [16384, 768], P(('grp', 'dp')), may hold values from -6 to 6
Outputs:
- update: float32 [2560, 768], P(('grp', 'dp'))
All inputs are finite; a program needn't handle non-finite values. Where the computation divides by a largest or mean magnitude, that divisor is 1e-20 or more.
Results may differ from a plain program's by a relative error of at most 0.013.
Values may be sent and summed in bfloat16 or wider, within the bound.
A program may use at most 64 MiB of HBM per device.

v0:
```python
import jax
import jax.numpy as jnp
from jax import lax
from jax.sharding import PartitionSpec as P

D = 2560
R = 768
BLK = 128
ITERS = 8


def newton_inverse(blocks):
    eye = jnp.eye(BLK, dtype=jnp.float32)
    trace = jnp.sum(blocks * eye, axis=(1, 2))
    damped = blocks + (0.1 * (trace / BLK + 1e-06))[:, None, None] * eye
    scale = 1.0 / jnp.max(jnp.sum(jnp.abs(damped), axis=2), axis=1)
    approx = scale[:, None, None] * eye
    for step in range(ITERS):
        product = jnp.einsum("nij,njk->nik", damped, approx, precision=lax.Precision.HIGHEST)
        approx = jnp.einsum(
            "nij,njk->nik", approx, 2.0 * eye - product, precision=lax.Precision.HIGHEST
        )
    return approx


def per_device(acts, cotangents):
    tokens = acts.shape[0]
    groups = lax.axis_size("grp")
    width_dp = lax.axis_size("dp")
    total = tokens * groups * width_dp
    in_blocks = D // BLK
    out_blocks = R // BLK
    all_blocks = in_blocks + out_blocks
    slots = (all_blocks + groups - 1) // groups
    padded_count = slots * groups
    x_blocks = acts.reshape(tokens, in_blocks, BLK)
    d_blocks = cotangents.reshape(tokens, out_blocks, BLK)
    fa = jnp.einsum("tbi,tbj->bij", x_blocks, x_blocks, preferred_element_type=jnp.float32) / total
    fg = jnp.einsum("tbi,tbj->bij", d_blocks, d_blocks, preferred_element_type=jnp.float32) / total
    filler = jnp.zeros((padded_count - all_blocks, BLK, BLK), jnp.float32)
    stacked = jnp.concatenate([fa, fg, filler], axis=0)
    owned = lax.psum_scatter(stacked, "grp", scatter_dimension=0, tiled=True)
    owned = lax.psum(owned, "dp")
    owned_inverse = newton_inverse(owned).astype(jnp.bfloat16)
    inverse16 = lax.all_gather(owned_inverse, "grp", axis=0, tiled=True)[:all_blocks]
    xpre = jnp.einsum(
        "tbi,bij->tbj", x_blocks, inverse16[:in_blocks], preferred_element_type=jnp.float32
    )
    xpre = xpre.astype(jnp.bfloat16).reshape(tokens, D)
    row_count = D // (groups * width_dp)
    mine = lax.psum_scatter(
        jnp.dot(xpre.T, cotangents, preferred_element_type=jnp.float32) / total,
        ("grp", "dp"),
        scatter_dimension=0,
        tiled=True,
    )
    out_inverse = inverse16[in_blocks:].astype(jnp.float32)
    natural = jnp.einsum(
        "rci,cij->rcj",
        mine.reshape(row_count, out_blocks, BLK),
        out_inverse,
        precision=lax.Precision.HIGHEST,
    ).reshape(row_count, R)
    quad = lax.psum(jnp.sum(natural * natural), ("grp", "dp")) / (D * R)
    return natural / jnp.sqrt(quad + 1e-06)


def solution(mesh):
    in_specs = (P(("grp", "dp"), None), P(("grp", "dp"), None))
    out_specs = P(("grp", "dp"), None)
    return jax.shard_map(
        per_device, mesh=mesh, in_specs=in_specs, out_specs=out_specs, check_vma=False
    )
```

profile of v0, /device:TPU:0, one launch (start us, length us, event | category | flops | bytes accessed | tf_op | source)
XLA Modules:
  0.0 350.6 jit_solution(1158352562578735457)
XLA Ops:
  6.5 0.0 reduce-scatter.3.cloned.1.call-start
  6.5 1.4 copy.28
  7.9 0.4 convolution_multiply_fusion.2
  8.3 3.0 copy.26
  11.3 0.8 convolution_multiply_fusion.1
  12.2 1.3 pad_maximum_fusion
  13.5 0.0 reduce-scatter.3.cloned.1.call-update
  13.5 0.0 all-reduce.2.cloned.1.call-start
  13.6 30.3 %reduce-scatter.3.cloned.1.call-done = f32[13,128,128]{2,1,0:T(8,128)} async-done(((f32[26,128,128]{2,1,0:T(8,128)}), f32[13,128,128]{2,1,0:T(8,128)}) %reduce-scatter.3.cloned.1.call-update) | async-done | bytes 851984 | tf_op jit(solution)/shard_map/reduce_scatter | solution.py:42
  43.9 0.0 all-reduce.2.cloned.1.call-update
  43.9 0.0 reduce-scatter.5.cloned.1.call-start
  44.0 0.6 fusion.10
  44.6 95.2 %all-reduce.2.cloned.1.call-done = f32[13,128,128]{2,1,0:T(8,128)} async-done(((f32[13,128,128]{2,1,0:T(8,128)}), f32[13,128,128]{2,1,0:T(8,128)}) %all-reduce.2.cloned.1.call-update) | async-done | bytes 851984 | tf_op jit(solution)/shard_map/psum | solution.py:43
  139.8 0.0 copy-start
  139.8 1.4 multiply_reduce_fusion
  141.2 1.5 abs_reduce_fusion
  142.8 0.1 reduce_max.9
  142.9 0.0 copy-start.1
  142.9 2.3 convolution_subtract_fusion.7
  145.2 1.0 fusion
  146.2 0.0 copy-done
  146.2 0.0 copy-done.1
  146.2 1.0 convolution_subtract_fusion.6
  147.3 0.9 fusion.12
  148.3 1.0 convolution_subtract_fusion.5
  149.3 0.9 fusion.13
  150.3 1.0 convolution_subtract_fusion.4
  151.3 0.9 fusion.14
  152.3 1.0 convolution_subtract_fusion.3
  153.3 0.9 fusion.15
  154.3 1.0 convolution_subtract_fusion.2
  155.3 1.1 fusion.16
  156.5 1.0 convolution_subtract_fusion.1
  157.5 0.9 fusion.17
  158.5 1.0 convolution_subtract_fusion
  159.5 0.9 convolution_convert_fusion.1
  160.5 12.2 %all_gather.3 = bf16[26,128,128]{2,1,0:T(8,128)(2,1)S(1)} all-gather(bf16[13,128,128]{2,1,0:T(8,128)(2,1)S(1)} %convolution_convert_fusion.1), channel_id=1, replica_groups=mesh['grp'=2,'dp'=16] {'grp'}, dimensions={0}, use_global_device_ids=true | all-gather | bytes 1277952 | tf_op jit(solution)/shard_map/all_gather | solution.py:45
  172.6 0.0 copy-start.2
  172.6 0.9 convolution_convert_fusion
  173.5 0.2 copy-done.2
  173.8 5.3 %convolution_multiply_fusion = f32[2560,768]{1,0:T(8,128)} fusion(bf16[512,2560]{0,1:T(8,128)(2,1)S(1)} %bitcast.54, bf16[512,768]{1,0:T(8,128)(2,1)S(1)} %copy-done.2), kind=kOutput, calls=%fused_computation | convolution fusion | flops 2015232000 | bytes 11272192 | tf_op jit(solution)/shard_map/dot_general | solution.py:52
  179.1 0.0 reduce-scatter.5.cloned.1.call-update
  179.1 121.5 %reduce-scatter.5.cloned.1.call-done = f32[80,768]{1,0:T(8,128)} async-done(((f32[2560,768]{1,0:T(8,128)}), f32[80,768]{1,0:T(8,128)}) %reduce-scatter.5.cloned.1.call-update) | async-done | bytes 245776 | tf_op jit(solution)/shard_map/reduce_scatter | solution.py:51
  300.5 1.9 multiply_reduce_fusion.1
  302.4 40.3 %psum.15 = f32[]{:T(128)} all-reduce(f32[]{:T(128)} %get-tuple-element.5), channel_id=1, replica_groups=mesh['grp'=2,'dp'=16] {'grp','dp'}, use_global_device_ids=true, to_apply=%region_7.0 | all-reduce | flops 1 | bytes 8 | tf_op jit(solution)/shard_map/psum | solution.py:64
  343.4 0.7 copy_bitcast_fusion
  (3 shorter events, 0.0 us)
Async XLA Ops:
  6.5 37.3 %reduce-scatter.3.cloned.1.call-start = ((), (), s32[]{:S(2)}) async-start(), calls=%async_computation.2 | async-start | bytes 2555904 | tf_op jit(solution)/shard_map/reduce_scatter | solution.py:42
  13.5 126.3 %all-reduce.2.cloned.1.call-start = ((), (), s32[]{:S(2)}) async-start(), calls=%async_computation.3 | async-start | bytes 1703936 | tf_op jit(solution)/shard_map/psum | solution.py:43
  43.9 256.6 %reduce-scatter.5.cloned.1.call-start = ((), (), s32[]{:S(2)}) async-start(), calls=%async_computation.4 | async-start | bytes 8110080 | tf_op jit(solution)/shard_map/reduce_scatter | solution.py:51
  139.8 6.4 %copy-start = (f32[13,128,128]{2,1,0:T(8,128)S(1)}, f32[13,128,128]{2,1,0:T(8,128)}, u32[]{:S(2)}) copy-start(f32[13,128,128]{2,1,0:T(8,128)} %all-reduce.2.cloned.1.call-done) | copy-start | bytes 2555908
  142.9 3.3 copy-start.1
  172.6 1.1 copy-start.2
Sparse Core Ops, SparseCore 0:
  13.6 30.1 reduce-scatter.2
  47.7 92.0 all-reduce.1
  179.2 121.2 reduce-scatter.4
where the time goes:
time: 351 us
  waiting for transfers between devices  247 us (70%)
  blocking collectives  52.4 us (15%)
  matrix products  26.7 us (8%)
  between operations  14 us (4%)
  other arithmetic  5.79 us (2%)
  local copies, waits for them, and re-layouts  4.65 us (1%)
    reduce_scatter x1, waiting for transfers between devices, per_device(): lax.psum_scatter(jnp.dot(xpre.T, cotangents, preferred_element_type=jnp.f...  121 us
    psum x1, waiting for transfers between devices, per_device(): owned = lax.psum(owned, 'dp')  95.2 us
    psum x1, blocking collectives, per_device(): quad = lax.psum(jnp.sum(natural * natural), ('grp', 'dp')) / (D * R)  40.3 us
    reduce_scatter x1, waiting for transfers between devices, per_device(): owned = lax.psum_scatter(stacked, 'grp', scatter_dimension=0, tiled=True)  30.3 us
    all_gather x1, blocking collectives, per_device(): lax.all_gather(owned_inverse, 'grp', axis=0, tiled=True)[:all_blocks]  12.2 us
    dot_general x8, matrix products, newton_inverse(): jnp.einsum('nij,njk->nik', damped, approx, precision=lax.Precision.HIGHEST)  9.59 us
    dot_general x8, matrix products, newton_inverse(): jnp.einsum('nij,njk->nik', approx, 2.0 * eye - product, precision=lax.Pre...  7.83 us
  transfers between devices with their start and end apart: 3, of which 3 were waited for; matrix products, arithmetic and copies ran while one was open for 0% of the time, Pallas kernels for 0%

commit v1 on v0

v1 whole, which is shorter than its diff:
```python
import functools

import jax
import jax.numpy as jnp
from jax import lax
from jax.experimental import pallas as pl
from jax.experimental.pallas import tpu as pltpu
from jax.sharding import PartitionSpec as P

D = 2560
R = 768
BLK = 128
ITERS = 8
NA = D // BLK
NG = R // BLK
QROWS = D // 4
QBLK = QROWS // BLK
HALF = QROWS // 2
CCOLS = R // 2
CBLK = CCOLS // BLK
SLOTS = 4
MESH = pl.DeviceIdType.MESH
F32 = jnp.float32
BF16 = jnp.bfloat16


def dot(a, b):
    return jnp.dot(a, b, preferred_element_type=F32)


def dot_t(a, b):
    return lax.dot_general(a, b, (((0,), (0,)), ((), ())), preferred_element_type=F32)


def split(a):
    hi = a.astype(BF16)
    return hi, (a - hi.astype(F32)).astype(BF16)


def dot3(a, b):
    ah, al = split(a)
    bh, bl = split(b)
    return dot(jnp.concatenate([ah, ah, al], axis=1), jnp.concatenate([bh, bl, bh], axis=0))


def kernel(
    groups, width, total, rows,
    x_ref, g_ref, out_ref,
    xt, fpart, f1recv, f2send, f2recv, f3send, f3recv,
    m1send, m1recv, macc, m2a, m2s, m2b, mq,
    inv_own, inv_a, inv_g, nat, fin_send, fin_recv, qsend, qrecv,
    f1_ss, f1_rs, f2_ss, f2_rs, f3_ss, f3_rs, m1_ss, m1_rs, ma_ss, ma_rs,
    mb_ss, mb_rs, inv_ss, inv_rs, fin_ss, fin_rs, q_ss, q_rs,
):
    devices = groups * width
    rest_n = devices // 8
    owners = devices // 4
    dp_rest = width // 4
    gi = lax.axis_index("grp")
    di = lax.axis_index("dp")
    me = gi * width + di
    core = lax.rem(di, 2)
    x = lax.rem(lax.div(di, 2), 2)
    y = lax.rem(gi, 2)
    q = 2 * y + x
    rest = lax.div(gi, 2) * dp_rest + lax.div(di, 4)

    def at(yy, xx, zz, cc):
        return (
            lax.div(zz, dp_rest) * 2 + yy,
            lax.rem(zz, dp_rest) * 4 + xx * 2 + cc,
        )

    def linear(d):
        return (lax.div(d, width), lax.rem(d, width))

    def rcopy(src, dst, ss, rs, dev):
        return pltpu.make_async_remote_copy(
            src_ref=src, dst_ref=dst, send_sem=ss, recv_sem=rs,
            device_id=dev, device_id_type=MESH,
        )

    barrier = pltpu.get_barrier_semaphore()

    @pl.loop(0, devices)
    def _(d):
        @pl.when(d != me)
        def _():
            pl.semaphore_signal(barrier, inc=1, device_id=linear(d), device_id_type=MESH)

    zero = jnp.zeros((BLK, BLK), BF16)

    @pl.loop(0, 4)
    def _(qq):
        for t in range(QBLK):
            b = qq * QBLK + t
            xb = x_ref[:, pl.ds(pl.multiple_of(b * BLK, BLK), BLK)]
            xbt = xb.T
            xt[b] = xbt
            fpart[t % 2, qq, t // 2] = dot(xbt, xb).astype(BF16)
        fpart[0, qq, 3] = zero
        fpart[1, qq, 3] = zero

    for c in range(NG):
        gb = g_ref[:, c * BLK:(c + 1) * BLK]
        fg = dot_t(gb, gb).astype(BF16)
        if c < 4:
            fpart[1, c, 2] = fg
        else:
            fpart[0, c - 4, 3] = fg

    pl.semaphore_wait(barrier, devices - 1)
    other = at(y, x, rest, 1 - core)
    f1 = rcopy(fpart.at[1 - core], f1recv, f1_ss.at[0], f1_rs.at[0], other)
    f1.start()

    g_other = g_ref[:, pl.ds(pl.multiple_of((1 - core) * CCOLS, BLK), CCOLS)]

    def m1_copy(qq):
        return rcopy(m1send.at[qq], m1recv.at[qq], m1_ss.at[qq], m1_rs.at[qq], other)

    @pl.loop(0, 4)
    def _(qq):
        for t in range(QBLK):
            m1send[qq, t * BLK:(t + 1) * BLK, :] = dot(xt[qq * QBLK + t], g_other).astype(BF16)
        m1_copy(qq).start()

    f1.wait_recv()

    def f1_sum(qq, s):
        return fpart[core, qq, s].astype(F32) + f1recv[qq, s].astype(F32)

    chips = [(y, 1 - x), (1 - y, x), (1 - y, 1 - x)]
    f2 = []
    for k, (yy, xx) in enumerate(chips):
        qq = 2 * yy + xx
        for s in range(SLOTS):
            f2send[k, s] = f1_sum(qq, s).astype(BF16)
        c2 = rcopy(f2send.at[k], f2recv.at[k], f2_ss.at[k], f2_rs.at[k], at(yy, xx, rest, core))
        c2.start()
        f2.append(c2)

    g_mine = g_ref[:, pl.ds(pl.multiple_of(core * CCOLS, BLK), CCOLS)]

    @pl.loop(0, 4)
    def _(qq):
        m1_copy(qq).wait_recv()
        for t in range(QBLK):
            part = dot(xt[qq * QBLK + t], g_mine)
            sl = slice(t * BLK, (t + 1) * BLK)
            macc[qq, sl, :] = (part + m1recv[qq, sl, :].astype(F32)).astype(BF16)

    at_x = at(y, 1 - x, rest, core)
    at_y = at(1 - y, x, rest, core)
    ma = []
    for i in range(2):
        for h in range(2):
            k = 2 * h + i
            quarter = 2 * i + (1 - x) if h == 0 else 2 * (1 - y) + i
            ca = rcopy(
                macc.at[quarter, pl.ds(h * HALF, HALF)], m2a.at[k],
                ma_ss.at[k], ma_rs.at[k], at_x if h == 0 else at_y,
            )
            ca.start()
            ma.append(ca)

    for c2 in f2:
        c2.wait_recv()
    for s in range(SLOTS):
        f = f1_sum(q, s)
        for k in range(3):
            f = f + f2recv[k, s].astype(F32)
        f3send[s] = f.astype(BF16)

    def f3_copy(s, src):
        return rcopy(f3send.at[s], f3recv.at[src], f3_ss.at[s], f3_rs.at[src], at(y, x, s, core))

    for s in range(SLOTS):
        @pl.when(rest != s)
        def _():
            f3_copy(s, rest).start()

    f3recv[rest] = f3send[lax.rem(rest, SLOTS)]

    @pl.when(rest < SLOTS)
    def _():
        @pl.loop(0, rest_n)
        def _(z):
            @pl.when(z != rest)
            def _():
                f3_copy(0, z).wait_recv()

    if rest_n > SLOTS:
        @pl.when(rest >= SLOTS)
        def _():
            @pl.loop(0, rest_n)
            def _(z):
                f3recv[z] = zero

    factor = f3recv[0].astype(F32)
    for z in range(1, rest_n):
        factor = factor + f3recv[z].astype(F32)
    factor = factor * (1.0 / total)

    eye = (
        lax.broadcasted_iota(jnp.int32, (BLK, BLK), 0)
        == lax.broadcasted_iota(jnp.int32, (BLK, BLK), 1)
    ).astype(F32)
    trace = jnp.sum(jnp.sum(factor * eye, axis=1, keepdims=True), axis=0, keepdims=True)
    damped = factor + (0.1 * (trace / BLK + 1e-06)) * eye
    peak = jnp.max(jnp.sum(jnp.abs(damped), axis=1, keepdims=True), axis=0, keepdims=True)
    scale = 1.0 / peak
    approx = scale * (2.0 * eye - scale * damped)
    for _ in range(ITERS - 5):
        approx = dot3(approx, 2.0 * eye - dot3(damped, approx))

    for ca in ma:
        ca.wait_recv()
    for i in range(2):
        for h in range(2):
            k = 2 * h + i
            quarter = 2 * i + x if h == 0 else 2 * y + i
            m2s[k] = (
                macc[quarter, h * HALF:(h + 1) * HALF, :].astype(F32) + m2a[k].astype(F32)
            ).astype(BF16)
    mb = [
        rcopy(m2s.at[1 - y], m2b.at[0], mb_ss.at[0], mb_rs.at[0], at_y),
        rcopy(m2s.at[2 + 1 - x], m2b.at[1], mb_ss.at[1], mb_rs.at[1], at_x),
    ]
    for cb in mb:
        cb.start()

    for _ in range(4):
        approx = dot3(approx, 2.0 * eye - dot3(damped, approx))
    inv_own[...] = approx.astype(BF16)

    slot = 2 * rest + core
    is_a = slot < QBLK
    is_g = jnp.logical_or(slot == QBLK, jnp.logical_and(slot == QBLK + 1, q < NG - 4))
    gidx = (slot - QBLK) * 4 + q
    ghalf = lax.div(gidx, CBLK)

    def a_copy(i, t):
        return rcopy(
            inv_own, inv_a.at[t], inv_ss.at[i], inv_rs.at[t],
            at(y, x, lax.div(i, 2), lax.rem(i, 2)),
        )

    def g_dev(i):
        chip = lax.div(i, rest_n)
        return at(lax.div(chip, 2), lax.rem(chip, 2), lax.rem(i, rest_n), ghalf)

    def g_copy(i, c):
        return rcopy(inv_own, inv_g.at[c], inv_ss.at[i], inv_rs.at[QBLK + c], g_dev(i))

    def not_me(i):
        gg, dd = g_dev(i)
        return gg * width + dd != me

    @pl.when(is_a)
    def _():
        @pl.loop(0, owners)
        def _(i):
            @pl.when(i != slot)
            def _():
                a_copy(i, slot).start()
        inv_a[slot] = inv_own[...]

    @pl.when(is_g)
    def _():
        @pl.loop(0, 4 * rest_n)
        def _(i):
            @pl.when(not_me(i))
            def _():
                g_copy(i, lax.rem(gidx, CBLK)).start()

        @pl.when(ghalf == core)
        def _():
            inv_g[lax.rem(gidx, CBLK)] = inv_own[...]

    for cb in mb:
        cb.wait_recv()
    for h in range(2):
        kept = m2s[y] if h == 0 else m2s[2 + x]
        mq[h * HALF:(h + 1) * HALF, :] = (
            (kept.astype(F32) + m2b[h].astype(F32)) * (1.0 / total)
        ).astype(BF16)

    for c in range(CBLK):
        @pl.when(jnp.logical_not(jnp.logical_and(is_g, gidx == core * CBLK + c)))
        def _():
            g_copy(0, c).wait_recv()
    for t in range(QBLK):
        @pl.when(slot != t)
        def _():
            a_copy(0, t).wait_recv()

    for t in range(QBLK):
        left = dot_t(inv_a[t], mq[t * BLK:(t + 1) * BLK, :])
        for c in range(CBLK):
            hi, lo = split(left[:, c * BLK:(c + 1) * BLK])
            ginv = inv_g[c]
            nat[t * BLK:(t + 1) * BLK, c * BLK:(c + 1) * BLK] = dot(hi, ginv) + dot(lo, ginv)

    def fin_copy(k, r):
        return rcopy(
            fin_send.at[k], fin_recv.at[r], fin_ss.at[k], fin_rs.at[r], linear(q * owners + k)
        )

    if rows % 16:
        fin_send[...] = jnp.zeros_like(fin_send)
    for k in range(owners):
        fin_send[k, :rows, :] = nat[k * rows:(k + 1) * rows, :].astype(BF16)

        @pl.when(q * owners + k != me)
        def _():
            fin_copy(k, slot).start()

        @pl.when(q * owners + k == me)
        def _():
            fin_recv[slot] = fin_send[k]

    from_me = lax.div(me, owners) == q

    @pl.loop(0, owners)
    def _(r):
        @pl.when(jnp.logical_not(jnp.logical_and(from_me, r == slot)))
        def _():
            fin_copy(0, r).wait_recv()

    square = jnp.zeros((1, 1), F32)
    natural = []
    for c in range(2):
        part = fin_recv[c].astype(F32)
        for z in range(1, rest_n):
            part = part + fin_recv[2 * z + c].astype(F32)
        part = part[:rows, :]
        natural.append(part)
        square = square + jnp.sum(
            jnp.sum(part * part, axis=0, keepdims=True), axis=1, keepdims=True
        )
    qsend[...] = jnp.broadcast_to(square, qsend.shape)
    qrecv[me] = qsend[...]

    def q_copy(d, src):
        return rcopy(qsend, qrecv.at[src], q_ss.at[d], q_rs.at[src], linear(d))

    @pl.loop(0, devices)
    def _(d):
        @pl.when(d != me)
        def _():
            q_copy(d, me).start()

    @pl.loop(0, devices)
    def _(d):
        @pl.when(d != me)
        def _():
            q_copy(0, d).wait_recv()

    quad = jnp.sum(qrecv[...], axis=0)[:1, :1] / (D * R)
    factor_out = lax.rsqrt(quad + 1e-06)
    for c in range(2):
        out_ref[:, c * CCOLS:(c + 1) * CCOLS] = natural[c] * factor_out

    f1.wait_send()
    for cp in f2 + ma + mb:
        cp.wait_send()

    @pl.loop(0, 4)
    def _(qq):
        m1_copy(qq).wait_send()

    for s in range(SLOTS):
        @pl.when(rest != s)
        def _():
            f3_copy(s, rest).wait_send()

    @pl.when(is_a)
    def _():
        @pl.loop(0, owners)
        def _(i):
            @pl.when(i != slot)
            def _():
                a_copy(i, 0).wait_send()

    @pl.when(is_g)
    def _():
        @pl.loop(0, 4 * rest_n)
        def _(i):
            @pl.when(not_me(i))
            def _():
                g_copy(i, 0).wait_send()

    @pl.loop(0, owners)
    def _(k):
        @pl.when(q * owners + k != me)
        def _():
            fin_copy(k, 0).wait_send()

    @pl.loop(0, devices)
    def _(d):
        @pl.when(d != me)
        def _():
            q_copy(d, 0).wait_send()


def per_device(acts, cotangents, groups, width):
    tokens = acts.shape[0]
    devices = groups * width
    rest_n = devices // 8
    owners = devices // 4
    rows = D // devices
    padded = (rows + 15) // 16 * 16
    blk = (BLK, BLK)
    sems = [1, 1, 3, 3, SLOTS, rest_n, 4, 4, 4, 4, 2, 2, max(owners, 4 * rest_n), QBLK + CBLK,
            owners, owners, devices, devices]
    vm = pltpu.VMEM
    return pl.pallas_call(
        functools.partial(kernel, groups, width, tokens * devices, rows),
        out_shape=jax.ShapeDtypeStruct((rows, R), F32),
        in_specs=[pl.BlockSpec(memory_space=pltpu.VMEM)] * 2,
        out_specs=pl.BlockSpec(memory_space=pltpu.VMEM),
        scratch_shapes=[
            vm((NA, BLK, tokens), BF16),
            vm((2, 4, SLOTS) + blk, BF16),
            vm((4, SLOTS) + blk, BF16),
            vm((3, SLOTS) + blk, BF16),
            vm((3, SLOTS) + blk, BF16),
            vm((SLOTS,) + blk, BF16),
            vm((rest_n,) + blk, BF16),
            vm((4, QROWS, CCOLS), BF16),
            vm((4, QROWS, CCOLS), BF16),
            vm((4, QROWS, CCOLS), BF16),
            vm((4, HALF, CCOLS), BF16),
            vm((4, HALF, CCOLS), BF16),
            vm((2, HALF, CCOLS), BF16),
            vm((QROWS, CCOLS), BF16),
            vm(blk, BF16),
            vm((QBLK,) + blk, BF16),
            vm((CBLK,) + blk, BF16),
            vm((QROWS, CCOLS), F32),
            vm((owners, padded, CCOLS), BF16),
            vm((owners, padded, CCOLS), BF16),
            vm((8, 128), F32),
            vm((devices, 8, 128), F32),
        ] + [pltpu.SemaphoreType.DMA((n,)) for n in sems],
        compiler_params=pltpu.CompilerParams(
            collective_id=0, has_side_effects=True, vmem_limit_bytes=48 * 1024 * 1024
        ),
    )(acts, cotangents)


def solution(mesh):
    groups, width = mesh.shape["grp"], mesh.shape["dp"]
    spec = P(("grp", "dp"), None)
    return jax.shard_map(
        functools.partial(per_device, groups=groups, width=width),
        mesh=mesh, in_specs=(spec, spec), out_specs=spec, check_vma=False,
    )
```

time: 351 us -> 72.8 us (0.21)
  waiting for transfers between devices: 247 us -> 0 us
  Pallas kernels: 0 us -> 69 us
  blocking collectives: 52.4 us -> 0 us
  matrix products: 26.7 us -> 0 us
  between operations: 14 us -> 0.01 us
  other arithmetic: 5.79 us -> 0 us
    reduce_scatter x2 -> x0, waiting for transfers between devices: 152 us -> none  [the longest x1 121 us: per_device(): lax.psum_scatter(jnp.dot(xpre.T, cotangents, preferred_element_type=jnp.f...]
    psum x1 -> x0, waiting for transfers between devices: 95.2 us -> none  [per_device(): owned = lax.psum(owned, 'dp')]
    pallas_call x0 -> x1, Pallas kernels: none -> 69 us  [per_device(): pl.pallas_call(functools.partial(kernel, groups, width, tokens * devices,...]
    psum x1 -> x0, blocking collectives: 40.3 us -> none  [per_device(): quad = lax.psum(jnp.sum(natural * natural), ('grp', 'dp')) / (D * R)]
    dot_general x21 -> x0, matrix products: 26.7 us -> none  [the longest x8 9.59 us: newton_inverse(): jnp.einsum('nij,njk->nik', damped, approx, precision=lax.Precision.HIGHEST)]
    all_gather x1 -> x0, blocking collectives: 12.2 us -> none  [per_device(): lax.all_gather(owned_inverse, 'grp', axis=0, tiled=True)[:all_blocks]]
  transfers between devices with their start and end apart: 3 -> 0, of which waited for: 3 -> 0; matrix products, arithmetic and copies ran while one was open for 0% -> 0% of each run, Pallas kernels for 0% -> 0%
where the time goes in v1:
time: 72.8 us; the launch traced here: 72.6 us
  Pallas kernels  69 us (95%)
  local copies, waits for them, and re-layouts  3.57 us (5%)
    pallas_call x1, Pallas kernels, per_device(): pl.pallas_call(functools.partial(kernel, groups, width, tokens * devices,...  69 us
    unnamed x5, local copies, waits for them, and re-layouts  3.57 us

profile of v1, /device:TPU:0, one launch (start us, length us, event | category | flops | bytes accessed | tf_op | source)
XLA Modules:
  0.0 72.6 jit_solution(7997997287663976588)
XLA Ops:
  0.0 0.0 copy-start
  0.0 1.7 %copy-done = bf16[512,2560]{1,0:T(8,128)(2,1)S(1)} copy-done((bf16[512,2560]{1,0:T(8,128)(2,1)S(1)}, bf16[512,2560]{1,0:T(8,128)(2,1)}, u32[]{:S(2)}) %copy-start) | copy-done | bytes 2621464
  1.7 0.0 copy-start.1
  1.7 1.1 %copy-done.1 = bf16[512,768]{1,0:T(8,128)(2,1)S(1)} copy-done((bf16[512,768]{1,0:T(8,128)(2,1)S(1)}, bf16[512,768]{1,0:T(8,128)(2,1)}, u32[]{:S(2)}) %copy-start.1) | copy-done | bytes 786456
  2.9 69.0 %shard_map.28 = f32[80,768]{1,0:T(8,128)S(1)} custom-call(bf16[512,2560]{1,0:T(8,128)(2,1)S(1)} %copy-done, bf16[512,768]{1,0:T(8,128)(2,1)S(1)} %copy-done.1), custom_call_target="tpu_custom_call" | custom-call | tf_op jit(solution)/shard_map/pallas_call | solution.py:418
  71.9 0.7 copy.4
Async XLA Ops:
  0.0 1.7 %copy-start = (bf16[512,2560]{1,0:T(8,128)(2,1)S(1)}, bf16[512,2560]{1,0:T(8,128)(2,1)}, u32[]{:S(2)}) copy-start(bf16[512,2560]{1,0:T(8,128)(2,1)} %x_ref.1) | copy-start | bytes 7864324
  1.7 1.1 %copy-start.1 = (bf16[512,768]{1,0:T(8,128)(2,1)S(1)}, bf16[512,768]{1,0:T(8,128)(2,1)}, u32[]{:S(2)}) copy-start(bf16[512,768]{1,0:T(8,128)(2,1)} %g_ref.1) | copy-start | bytes 2359300

commit v2 on v1

--- a/solution.py
+++ b/solution.py
@@ -45,16 +45,19 @@
 
 def kernel(
     groups, width, total, rows,
-    x_ref, g_ref, out_ref,
-    xt, fpart, f1recv, f2send, f2recv, f3send, f3recv,
+    x_hbm, g_hbm, out_ref,
+    x_ref, g_ref, xt, fpart, f1recv, f2send, f2recv, f3send, f3recv,
     m1send, m1recv, macc, m2a, m2s, m2b, mq,
-    inv_own, inv_a, inv_g, nat, fin_send, fin_recv, qsend, qrecv,
+    zsend, zrecv, inv_own, inv_a, inv_g, nat, fin_send, fin_recv, qsend, q1recv, q2recv,
+    in_sem,
     f1_ss, f1_rs, f2_ss, f2_rs, f3_ss, f3_rs, m1_ss, m1_rs, ma_ss, ma_rs,
-    mb_ss, mb_rs, inv_ss, inv_rs, fin_ss, fin_rs, q_ss, q_rs,
+    mb_ss, mb_rs, z_ss, z_rs, inv_ss, inv_rs, fin_ss, fin_rs, q1_ss, q1_rs, q2_ss, q2_rs,
 ):
     devices = groups * width
     rest_n = devices // 8
     owners = devices // 4
+    zslots = zsend.shape[1]
+    pieces = fin_send.shape[0] // zslots
     dp_rest = width // 4
     gi = lax.axis_index("grp")
     di = lax.axis_index("dp")
@@ -80,6 +83,14 @@
             device_id=dev, device_id_type=MESH,
         )
 
+    g_in = pltpu.make_async_copy(g_hbm, g_ref, in_sem.at[4])
+    g_in.start()
+    x_in = []
+    for i in range(4):
+        cols = pl.ds(i * QROWS, QROWS)
+        x_in.append(pltpu.make_async_copy(x_hbm.at[:, cols], x_ref.at[:, cols], in_sem.at[i]))
+        x_in[i].start()
+
     barrier = pltpu.get_barrier_semaphore()
 
     @pl.loop(0, devices)
@@ -89,18 +100,7 @@
             pl.semaphore_signal(barrier, inc=1, device_id=linear(d), device_id_type=MESH)
 
     zero = jnp.zeros((BLK, BLK), BF16)
-
-    @pl.loop(0, 4)
-    def _(qq):
-        for t in range(QBLK):
-            b = qq * QBLK + t
-            xb = x_ref[:, pl.ds(pl.multiple_of(b * BLK, BLK), BLK)]
-            xbt = xb.T
-            xt[b] = xbt
-            fpart[t % 2, qq, t // 2] = dot(xbt, xb).astype(BF16)
-        fpart[0, qq, 3] = zero
-        fpart[1, qq, 3] = zero
-
+    g_in.wait()
     for c in range(NG):
         gb = g_ref[:, c * BLK:(c + 1) * BLK]
         fg = dot_t(gb, gb).astype(BF16)
@@ -108,6 +108,19 @@
             fpart[1, c, 2] = fg
         else:
             fpart[0, c - 4, 3] = fg
+    for c in range(4):
+        fpart[1, c, 3] = zero
+        if c >= NG - 4:
+            fpart[0, c, 3] = zero
+
+    for qq in range(4):
+        x_in[qq].wait()
+        for t in range(QBLK):
+            b = qq * QBLK + t
+            xb = x_ref[:, b * BLK:(b + 1) * BLK]
+            xbt = xb.T
+            xt[b] = xbt
+            fpart[t % 2, qq, t // 2] = dot(xbt, xb).astype(BF16)
 
     pl.semaphore_wait(barrier, devices - 1)
     other = at(y, x, rest, 1 - core)
@@ -286,6 +299,22 @@
             (kept.astype(F32) + m2b[h].astype(F32)) * (1.0 / total)
         ).astype(BF16)
 
+    for i in range(zslots * rest_n):
+        t, c = divmod(i, CBLK)
+        tile = zero if t >= QBLK else mq[t * BLK:(t + 1) * BLK, c * BLK:(c + 1) * BLK]
+        zsend[i % rest_n, i // rest_n] = tile
+
+    def z_copy(dst, src):
+        return rcopy(zsend.at[dst], zrecv.at[src], z_ss.at[dst], z_rs.at[src], at(y, x, dst, core))
+
+    @pl.loop(0, rest_n)
+    def _(z):
+        @pl.when(z != rest)
+        def _():
+            z_copy(z, rest).start()
+
+    zrecv[rest] = zsend[rest]
+
     for c in range(CBLK):
         @pl.when(jnp.logical_not(jnp.logical_and(is_g, gidx == core * CBLK + c)))
         def _():
@@ -295,72 +324,122 @@
         def _():
             a_copy(0, t).wait_recv()
 
-    for t in range(QBLK):
-        left = dot_t(inv_a[t], mq[t * BLK:(t + 1) * BLK, :])
-        for c in range(CBLK):
-            hi, lo = split(left[:, c * BLK:(c + 1) * BLK])
-            ginv = inv_g[c]
-            nat[t * BLK:(t + 1) * BLK, c * BLK:(c + 1) * BLK] = dot(hi, ginv) + dot(lo, ginv)
-
-    def fin_copy(k, r):
-        return rcopy(
-            fin_send.at[k], fin_recv.at[r], fin_ss.at[k], fin_rs.at[r], linear(q * owners + k)
-        )
-
-    if rows % 16:
-        fin_send[...] = jnp.zeros_like(fin_send)
-    for k in range(owners):
-        fin_send[k, :rows, :] = nat[k * rows:(k + 1) * rows, :].astype(BF16)
-
-        @pl.when(q * owners + k != me)
-        def _():
-            fin_copy(k, slot).start()
-
-        @pl.when(q * owners + k == me)
-        def _():
-            fin_recv[slot] = fin_send[k]
-
-    from_me = lax.div(me, owners) == q
-
-    @pl.loop(0, owners)
-    def _(r):
-        @pl.when(jnp.logical_not(jnp.logical_and(from_me, r == slot)))
-        def _():
-            fin_copy(0, r).wait_recv()
+    @pl.loop(0, rest_n)
+    def _(z):
+        @pl.when(z != rest)
+        def _():
+            z_copy(0, z).wait_recv()
 
     square = jnp.zeros((1, 1), F32)
-    natural = []
-    for c in range(2):
-        part = fin_recv[c].astype(F32)
+    for k in range(zslots):
+        tile = k * rest_n + rest
+        m = zrecv[0, k].astype(F32)
         for z in range(1, rest_n):
-            part = part + fin_recv[2 * z + c].astype(F32)
-        part = part[:rows, :]
-        natural.append(part)
+            m = m + zrecv[z, k].astype(F32)
+        left = dot_t(inv_a[jnp.minimum(lax.div(tile, CBLK), QBLK - 1)], m.astype(BF16))
+        hi, lo = split(left)
+        ginv = inv_g[lax.rem(tile, CBLK)]
+        part = dot(hi, ginv) + dot(lo, ginv)
+        nat[k] = part
         square = square + jnp.sum(
             jnp.sum(part * part, axis=0, keepdims=True), axis=1, keepdims=True
         )
-    qsend[...] = jnp.broadcast_to(square, qsend.shape)
-    qrecv[me] = qsend[...]
-
-    def q_copy(d, src):
-        return rcopy(qsend, qrecv.at[src], q_ss.at[d], q_rs.at[src], linear(d))
-
-    @pl.loop(0, devices)
-    def _(d):
-        @pl.when(d != me)
-        def _():
-            q_copy(d, me).start()
-
-    @pl.loop(0, devices)
-    def _(d):
-        @pl.when(d != me)
-        def _():
-            q_copy(0, d).wait_recv()
-
-    quad = jnp.sum(qrecv[...], axis=0)[:1, :1] / (D * R)
+    qsend[0] = jnp.broadcast_to(square, (8, 128))
+
+    def q1_copy(p, src):
+        return rcopy(
+            qsend.at[0], q1recv.at[src], q1_ss.at[p], q1_rs.at[src],
+            at(lax.div(p, 4), lax.rem(lax.div(p, 2), 2), rest, lax.rem(p, 2)),
+        )
+
+    def q2_copy(z, src):
+        return rcopy(qsend.at[1], q2recv.at[src], q2_ss.at[z], q2_rs.at[src], at(y, x, z, core))
+
+    plane = 2 * q + core
+
+    def others(n, mine, body):
+        @pl.loop(0, n)
+        def _(p):
+            @pl.when(p != mine)
+            def _():
+                body(p)
+
+    others(8, plane, lambda p: q1_copy(p, plane).start())
+    q1recv[plane] = qsend[0]
+
+    def each_piece(body):
+        for i in range(QBLK * CBLK):
+            t, c = divmod(i, CBLK)
+
+            @pl.when(rest == i % rest_n)
+            def _():
+                first = t * BLK // rows
+                for k in range(first, min(owners, ((t + 1) * BLK + rows - 1) // rows)):
+                    lo, hi = max(t * BLK, k * rows), min((t + 1) * BLK, (k + 1) * rows)
+                    late = 0 if lo == k * rows else 1
+                    body(i, t, c, k, lo, hi, late, i // rest_n * pieces + k - first)
+
+    def fin_copy(j, c, late, k):
+        return rcopy(
+            fin_send.at[j], fin_recv.at[core * CBLK + c, late], fin_ss.at[j],
+            fin_rs.at[2 * (core * CBLK + c) + late], linear(q * owners + k),
+        )
+
+    def send_piece(i, t, c, k, lo, hi, late, j):
+        parts = [nat[i // rest_n, lo - t * BLK:hi - t * BLK, :]]
+        if lo > k * rows:
+            parts.insert(0, jnp.zeros((lo - k * rows, BLK), F32))
+        tail = fin_send.shape[1] - (hi - k * rows)
+        if tail:
+            parts.append(jnp.zeros((tail, BLK), F32))
+        fin_send[j] = (jnp.concatenate(parts, axis=0) if len(parts) > 1 else parts[0]).astype(BF16)
+
+        @pl.when(q * owners + k != me)
+        def _():
+            fin_copy(j, c, late, k).start()
+
+        @pl.when(q * owners + k == me)
+        def _():
+            fin_recv[core * CBLK + c, late] = fin_send[j]
+
+    each_piece(send_piece)
+
+    others(8, plane, lambda p: q1_copy(0, p).wait_recv())
+    qsend[1] = jnp.sum(q1recv[...], axis=0)
+    others(rest_n, rest, lambda z: q2_copy(z, rest).start())
+    q2recv[rest] = qsend[1]
+
+    k_me = lax.rem(me, owners)
+    t_me = lax.div(k_me * rows, BLK)
+    straddles = lax.div(k_me * rows + rows - 1, BLK) > t_me
+    mine_here = lax.div(me, owners) == q
+    for late in range(2):
+        for c in range(NG):
+            from_me = jnp.logical_and(
+                jnp.logical_and(mine_here, core == c // CBLK),
+                lax.rem(CBLK * (t_me + late) + c % CBLK, rest_n) == rest,
+            )
+            incoming = jnp.logical_not(from_me)
+            if late:
+                incoming = jnp.logical_and(straddles, incoming)
+
+                @pl.when(jnp.logical_not(straddles))
+                def _():
+                    fin_recv[c, 1] = jnp.zeros(fin_recv.shape[2:], BF16)
+
+            @pl.when(incoming)
+            def _():
+                pltpu.make_async_remote_copy(
+                    src_ref=fin_send.at[0], dst_ref=fin_recv.at[c, late], send_sem=fin_ss.at[0],
+                    recv_sem=fin_rs.at[2 * c + late], device_id=other, device_id_type=MESH,
+                ).wait_recv()
+
+    others(rest_n, rest, lambda z: q2_copy(0, z).wait_recv())
+    quad = jnp.sum(q2recv[...], axis=0)[:1, :1] / (D * R)
     factor_out = lax.rsqrt(quad + 1e-06)
-    for c in range(2):
-        out_ref[:, c * CCOLS:(c + 1) * CCOLS] = natural[c] * factor_out
+    for c in range(NG):
+        natural = fin_recv[c, 0].astype(F32) + fin_recv[c, 1].astype(F32)
+        out_ref[:, c * BLK:(c + 1) * BLK] = natural[:rows, :] * factor_out
 
     f1.wait_send()
     for cp in f2 + ma + mb:
@@ -391,17 +470,16 @@
             def _():
                 g_copy(i, 0).wait_send()
 
-    @pl.loop(0, owners)
-    def _(k):
+    others(rest_n, rest, lambda z: z_copy(z, 0).wait_send())
+    others(8, plane, lambda p: q1_copy(p, 0).wait_send())
+    others(rest_n, rest, lambda z: q2_copy(z, 0).wait_send())
+
+    def wait_piece(i, t, c, k, lo, hi, late, j):
         @pl.when(q * owners + k != me)
         def _():
-            fin_copy(k, 0).wait_send()
-
-    @pl.loop(0, devices)
-    def _(d):
-        @pl.when(d != me)
-        def _():
-            q_copy(d, 0).wait_send()
+            fin_copy(j, c, late, k).wait_send()
+
+    each_piece(wait_piece)
 
 
 def per_device(acts, cotangents, groups, width):
@@ -412,15 +490,21 @@
     rows = D // devices
     padded = (rows + 15) // 16 * 16
     blk = (BLK, BLK)
-    sems = [1, 1, 3, 3, SLOTS, rest_n, 4, 4, 4, 4, 2, 2, max(owners, 4 * rest_n), QBLK + CBLK,
-            owners, owners, devices, devices]
+    zslots = (QBLK * CBLK + rest_n - 1) // rest_n
+    pieces = max(
+        ((t + 1) * BLK + rows - 1) // rows - t * BLK // rows for t in range(QBLK)
+    )
+    sems = [5, 1, 1, 3, 3, SLOTS, rest_n, 4, 4, 4, 4, 2, 2, rest_n, rest_n, max(owners, 4 * rest_n),
+            QBLK + CBLK, zslots * pieces, 2 * NG, 8, 8, rest_n, rest_n]
     vm = pltpu.VMEM
     return pl.pallas_call(
         functools.partial(kernel, groups, width, tokens * devices, rows),
         out_shape=jax.ShapeDtypeStruct((rows, R), F32),
-        in_specs=[pl.BlockSpec(memory_space=pltpu.VMEM)] * 2,
+        in_specs=[pl.BlockSpec(memory_space=pl.ANY)] * 2,
         out_specs=pl.BlockSpec(memory_space=pltpu.VMEM),
         scratch_shapes=[
+            vm((tokens, D), BF16),
+            vm((tokens, R), BF16),
             vm((NA, BLK, tokens), BF16),
             vm((2, 4, SLOTS) + blk, BF16),
             vm((4, SLOTS) + blk, BF16),
@@ -435,14 +519,17 @@
             vm((4, HALF, CCOLS), BF16),
             vm((2, HALF, CCOLS), BF16),
             vm((QROWS, CCOLS), BF16),
+            vm((rest_n, zslots) + blk, BF16),
+            vm((rest_n, zslots) + blk, BF16),
             vm(blk, BF16),
             vm((QBLK,) + blk, BF16),
             vm((CBLK,) + blk, BF16),
-            vm((QROWS, CCOLS), F32),
-            vm((owners, padded, CCOLS), BF16),
-            vm((owners, padded, CCOLS), BF16),
-            vm((8, 128), F32),
-            vm((devices, 8, 128), F32),
+            vm((zslots,) + blk, F32),
+            vm((zslots * pieces, padded, BLK), BF16),
+            vm((NG, 2, padded, BLK), BF16),
+            vm((2, 8, 128), F32),
+            vm((8, 8, 128), F32),
+            vm((rest_n, 8, 128), F32),
         ] + [pltpu.SemaphoreType.DMA((n,)) for n in sems],
         compiler_params=pltpu.CompilerParams(
             collective_id=0, has_side_effects=True, vmem_limit_bytes=48 * 1024 * 1024

time: 72.8 us -> 67.5 us (0.927)
  Pallas kernels: 69 us -> 63.8 us
    pallas_call x1, Pallas kernels: 69 us -> 63.8 us  [per_device(): pl.pallas_call(functools.partial(kernel, groups, width, tokens * devices,...]
where the time goes in v2:
time: 67.5 us; the launch traced here: 67.4 us
  Pallas kernels  63.8 us (95%)
  local copies, waits for them, and re-layouts  3.57 us (5%)
    pallas_call x1, Pallas kernels, per_device(): pl.pallas_call(functools.partial(kernel, groups, width, tokens * devices,...  63.8 us
    unnamed x5, local copies, waits for them, and re-layouts  3.57 us

profile of v2, /device:TPU:0, one launch (start us, length us, event | category | flops | bytes accessed | tf_op | source)
XLA Modules:
  0.0 67.4 jit_solution(2556961010161695769)
XLA Ops:
  0.0 0.0 copy-start
  0.0 1.7 %copy-done = bf16[512,2560]{1,0:T(8,128)(2,1)S(1)} copy-done((bf16[512,2560]{1,0:T(8,128)(2,1)S(1)}, bf16[512,2560]{1,0:T(8,128)(2,1)}, u32[]{:S(2)}) %copy-start) | copy-done | bytes 2621464
  1.7 0.0 copy-start.1
  1.7 1.1 %copy-done.1 = bf16[512,768]{1,0:T(8,128)(2,1)S(1)} copy-done((bf16[512,768]{1,0:T(8,128)(2,1)S(1)}, bf16[512,768]{1,0:T(8,128)(2,1)}, u32[]{:S(2)}) %copy-start.1) | copy-done | bytes 786456
  2.9 63.8 %shard_map.28 = f32[80,768]{1,0:T(8,128)S(1)} custom-call(bf16[512,2560]{1,0:T(8,128)(2,1)S(1)} %copy-done, bf16[512,768]{1,0:T(8,128)(2,1)S(1)} %copy-done.1), custom_call_target="tpu_custom_call" | custom-call | tf_op jit(solution)/shard_map/pallas_call | solution.py:500
  66.7 0.7 %copy.4 = f32[80,768]{1,0:T(8,128)} copy(f32[80,768]{1,0:T(8,128)S(1)} %shard_map.28) | data formatting | bytes 491520
Async XLA Ops:
  0.0 1.7 %copy-start = (bf16[512,2560]{1,0:T(8,128)(2,1)S(1)}, bf16[512,2560]{1,0:T(8,128)(2,1)}, u32[]{:S(2)}) copy-start(bf16[512,2560]{1,0:T(8,128)(2,1)} %x_hbm.1) | copy-start | bytes 7864324
  1.7 1.1 %copy-start.1 = (bf16[512,768]{1,0:T(8,128)(2,1)S(1)}, bf16[512,768]{1,0:T(8,128)(2,1)}, u32[]{:S(2)}) copy-start(bf16[512,768]{1,0:T(8,128)(2,1)} %g_hbm.1) | copy-start | bytes 2359300

commit v3 on v2

--- a/solution.py
+++ b/solution.py
@@ -56,6 +56,7 @@
     devices = groups * width
     rest_n = devices // 8
     owners = devices // 4
+    half_n = devices // 2
     zslots = zsend.shape[1]
     pieces = fin_send.shape[0] // zslots
     dp_rest = width // 4
@@ -93,11 +94,18 @@
 
     barrier = pltpu.get_barrier_semaphore()
 
-    @pl.loop(0, devices)
-    def _(d):
-        @pl.when(d != me)
-        def _():
-            pl.semaphore_signal(barrier, inc=1, device_id=linear(d), device_id_type=MESH)
+    def greet(dev):
+        pl.semaphore_signal(barrier, inc=1, device_id=dev, device_id_type=MESH)
+
+    greet(at(y, x, rest, 1 - core))
+    for yy, xx in ((y, 1 - x), (1 - y, x), (1 - y, 1 - x)):
+        greet(at(yy, xx, rest, core))
+
+    @pl.loop(0, rest_n)
+    def _(z):
+        @pl.when(z != rest)
+        def _():
+            greet(at(y, x, z, core))
 
     zero = jnp.zeros((BLK, BLK), BF16)
     g_in.wait()
@@ -113,16 +121,16 @@
         if c >= NG - 4:
             fpart[0, c, 3] = zero
 
-    for qq in range(4):
-        x_in[qq].wait()
-        for t in range(QBLK):
-            b = qq * QBLK + t
+    for part in range(4):
+        x_in[part].wait()
+        for b in range(part * QBLK, (part + 1) * QBLK):
+            qq, t = b // (2 * QBLK) * 2 + b % 2, b % (2 * QBLK) // 2
             xb = x_ref[:, b * BLK:(b + 1) * BLK]
             xbt = xb.T
-            xt[b] = xbt
+            xt[qq * QBLK + t] = xbt
             fpart[t % 2, qq, t // 2] = dot(xbt, xb).astype(BF16)
 
-    pl.semaphore_wait(barrier, devices - 1)
+    pl.semaphore_wait(barrier, rest_n + 3)
     other = at(y, x, rest, 1 - core)
     f1 = rcopy(fpart.at[1 - core], f1recv, f1_ss.at[0], f1_rs.at[0], other)
     f1.start()
@@ -302,7 +310,7 @@
     for i in range(zslots * rest_n):
         t, c = divmod(i, CBLK)
         tile = zero if t >= QBLK else mq[t * BLK:(t + 1) * BLK, c * BLK:(c + 1) * BLK]
-        zsend[i % rest_n, i // rest_n] = tile
+        zsend[i // zslots, i % zslots] = tile
 
     def z_copy(dst, src):
         return rcopy(zsend.at[dst], zrecv.at[src], z_ss.at[dst], z_rs.at[src], at(y, x, dst, core))
@@ -332,7 +340,7 @@
 
     square = jnp.zeros((1, 1), F32)
     for k in range(zslots):
-        tile = k * rest_n + rest
+        tile = rest * zslots + k
         m = zrecv[0, k].astype(F32)
         for z in range(1, rest_n):
             m = m + zrecv[z, k].astype(F32)
@@ -368,37 +376,40 @@
     q1recv[plane] = qsend[0]
 
     def each_piece(body):
-        for i in range(QBLK * CBLK):
-            t, c = divmod(i, CBLK)
-
-            @pl.when(rest == i % rest_n)
-            def _():
-                first = t * BLK // rows
-                for k in range(first, min(owners, ((t + 1) * BLK + rows - 1) // rows)):
-                    lo, hi = max(t * BLK, k * rows), min((t + 1) * BLK, (k + 1) * rows)
-                    late = 0 if lo == k * rows else 1
-                    body(i, t, c, k, lo, hi, late, i // rest_n * pieces + k - first)
+        for xx in range(2):
+            for i in range(QBLK * CBLK):
+                t, c = divmod(i, CBLK)
+                top = (2 * t + xx) * BLK
+
+                @pl.when(jnp.logical_and(x == xx, rest == i // zslots))
+                def _():
+                    first = top // rows
+                    for k in range(first, (top + BLK + rows - 1) // rows):
+                        lo, hi = max(top, k * rows), min(top + BLK, (k + 1) * rows)
+                        late = 0 if lo == k * rows else 1
+                        body(i % zslots, c, k, lo - k * rows, lo - top, hi - lo, late,
+                             i % zslots * pieces + k - first)
 
     def fin_copy(j, c, late, k):
         return rcopy(
             fin_send.at[j], fin_recv.at[core * CBLK + c, late], fin_ss.at[j],
-            fin_rs.at[2 * (core * CBLK + c) + late], linear(q * owners + k),
+            fin_rs.at[2 * (core * CBLK + c) + late], linear(y * half_n + k),
         )
 
-    def send_piece(i, t, c, k, lo, hi, late, j):
-        parts = [nat[i // rest_n, lo - t * BLK:hi - t * BLK, :]]
-        if lo > k * rows:
-            parts.insert(0, jnp.zeros((lo - k * rows, BLK), F32))
-        tail = fin_send.shape[1] - (hi - k * rows)
+    def send_piece(slot_k, c, k, above, start, count, late, j):
+        parts = [nat[slot_k, start:start + count, :]]
+        if above:
+            parts.insert(0, jnp.zeros((above, BLK), F32))
+        tail = fin_send.shape[1] - above - count
         if tail:
             parts.append(jnp.zeros((tail, BLK), F32))
         fin_send[j] = (jnp.concatenate(parts, axis=0) if len(parts) > 1 else parts[0]).astype(BF16)
 
-        @pl.when(q * owners + k != me)
+        @pl.when(y * half_n + k != me)
         def _():
             fin_copy(j, c, late, k).start()
 
-        @pl.when(q * owners + k == me)
+        @pl.when(y * half_n + k == me)
         def _():
             fin_recv[core * CBLK + c, late] = fin_send[j]
 
@@ -409,15 +420,18 @@
     others(rest_n, rest, lambda z: q2_copy(z, rest).start())
     q2recv[rest] = qsend[1]
 
-    k_me = lax.rem(me, owners)
+    k_me = lax.rem(me, half_n)
     t_me = lax.div(k_me * rows, BLK)
     straddles = lax.div(k_me * rows + rows - 1, BLK) > t_me
-    mine_here = lax.div(me, owners) == q
+    mine_here = lax.div(me, half_n) == y
     for late in range(2):
         for c in range(NG):
             from_me = jnp.logical_and(
                 jnp.logical_and(mine_here, core == c // CBLK),
-                lax.rem(CBLK * (t_me + late) + c % CBLK, rest_n) == rest,
+                jnp.logical_and(
+                    lax.rem(t_me + late, 2) == x,
+                    lax.div(CBLK * lax.div(t_me + late, 2) + c % CBLK, zslots) == rest,
+                ),
             )
             incoming = jnp.logical_not(from_me)
             if late:
@@ -474,8 +488,8 @@
     others(8, plane, lambda p: q1_copy(p, 0).wait_send())
     others(rest_n, rest, lambda z: q2_copy(z, 0).wait_send())
 
-    def wait_piece(i, t, c, k, lo, hi, late, j):
-        @pl.when(q * owners + k != me)
+    def wait_piece(slot_k, c, k, above, start, count, late, j):
+        @pl.when(y * half_n + k != me)
         def _():
             fin_copy(j, c, late, k).wait_send()
 
@@ -492,7 +506,7 @@
     blk = (BLK, BLK)
     zslots = (QBLK * CBLK + rest_n - 1) // rest_n
     pieces = max(
-        ((t + 1) * BLK + rows - 1) // rows - t * BLK // rows for t in range(QBLK)
+        ((t + 1) * BLK + rows - 1) // rows - t * BLK // rows for t in range(2 * QBLK)
     )
     sems = [5, 1, 1, 3, 3, SLOTS, rest_n, 4, 4, 4, 4, 2, 2, rest_n, rest_n, max(owners, 4 * rest_n),
             QBLK + CBLK, zslots * pieces, 2 * NG, 8, 8, rest_n, rest_n]

time: 67.5 us -> 60.5 us (0.90)
  Pallas kernels: 63.8 us -> 56.7 us
    pallas_call x1, Pallas kernels: 63.8 us -> 56.7 us  [per_device(): pl.pallas_call(functools.partial(kernel, groups, width, tokens * devices,...]
where the time goes in v3:
time: 60.5 us; the launch traced here: 60.3 us
  Pallas kernels  56.7 us (94%)
  local copies, waits for them, and re-layouts  3.57 us (6%)
    pallas_call x1, Pallas kernels, per_device(): pl.pallas_call(functools.partial(kernel, groups, width, tokens * devices,...  56.7 us
    unnamed x5, local copies, waits for them, and re-layouts  3.57 us

profile of v3, /device:TPU:0, one launch (start us, length us, event | category | flops | bytes accessed | tf_op | source)
XLA Modules:
  0.0 60.3 jit_solution(2645095453057309668)
XLA Ops:
  0.0 0.0 copy-start
  0.0 1.7 %copy-done = bf16[512,2560]{1,0:T(8,128)(2,1)S(1)} copy-done((bf16[512,2560]{1,0:T(8,128)(2,1)S(1)}, bf16[512,2560]{1,0:T(8,128)(2,1)}, u32[]{:S(2)}) %copy-start) | copy-done | bytes 2621464
  1.7 0.0 copy-start.1
  1.7 1.1 %copy-done.1 = bf16[512,768]{1,0:T(8,128)(2,1)S(1)} copy-done((bf16[512,768]{1,0:T(8,128)(2,1)S(1)}, bf16[512,768]{1,0:T(8,128)(2,1)}, u32[]{:S(2)}) %copy-start.1) | copy-done | bytes 786456
  2.9 56.7 %shard_map.28 = f32[80,768]{1,0:T(8,128)S(1)} custom-call(bf16[512,2560]{1,0:T(8,128)(2,1)S(1)} %copy-done, bf16[512,768]{1,0:T(8,128)(2,1)S(1)} %copy-done.1), custom_call_target="tpu_custom_call" | custom-call | tf_op jit(solution)/shard_map/pallas_call | solution.py:514
  59.6 0.7 %copy.4 = f32[80,768]{1,0:T(8,128)} copy(f32[80,768]{1,0:T(8,128)S(1)} %shard_map.28) | data formatting | bytes 491520
Async XLA Ops:
  0.0 1.7 %copy-start = (bf16[512,2560]{1,0:T(8,128)(2,1)S(1)}, bf16[512,2560]{1,0:T(8,128)(2,1)}, u32[]{:S(2)}) copy-start(bf16[512,2560]{1,0:T(8,128)(2,1)} %x_hbm.1) | copy-start | bytes 7864324
  1.7 1.1 %copy-start.1 = (bf16[512,768]{1,0:T(8,128)(2,1)S(1)}, bf16[512,768]{1,0:T(8,128)(2,1)}, u32[]{:S(2)}) copy-start(bf16[512,768]{1,0:T(8,128)(2,1)} %g_hbm.1) | copy-start | bytes 2359300

commit v4 on v3

--- a/solution.py
+++ b/solution.py
@@ -140,8 +140,9 @@
     def m1_copy(qq):
         return rcopy(m1send.at[qq], m1recv.at[qq], m1_ss.at[qq], m1_rs.at[qq], other)
 
-    @pl.loop(0, 4)
-    def _(qq):
+    @pl.loop(1, 5)
+    def _(turn):
+        qq = lax.rem(q + turn, 4)
         for t in range(QBLK):
             m1send[qq, t * BLK:(t + 1) * BLK, :] = dot(xt[qq * QBLK + t], g_other).astype(BF16)
         m1_copy(qq).start()
@@ -163,27 +164,36 @@
 
     g_mine = g_ref[:, pl.ds(pl.multiple_of(core * CCOLS, BLK), CCOLS)]
 
-    @pl.loop(0, 4)
-    def _(qq):
+    at_x = at(y, 1 - x, rest, core)
+    at_y = at(1 - y, x, rest, core)
+
+    def ma_copy(i, h):
+        quarter = 2 * i + (1 - x) if h == 0 else 2 * (1 - y) + i
+        k = 2 * h + i
+        return rcopy(
+            macc.at[quarter, pl.ds(h * HALF, HALF)], m2a.at[k],
+            ma_ss.at[k], ma_rs.at[k], at_x if h == 0 else at_y,
+        )
+
+    @pl.loop(1, 5)
+    def _(turn):
+        qq = lax.rem(q + turn, 4)
         m1_copy(qq).wait_recv()
         for t in range(QBLK):
             part = dot(xt[qq * QBLK + t], g_mine)
             sl = slice(t * BLK, (t + 1) * BLK)
             macc[qq, sl, :] = (part + m1recv[qq, sl, :].astype(F32)).astype(BF16)
-
-    at_x = at(y, 1 - x, rest, core)
-    at_y = at(1 - y, x, rest, core)
-    ma = []
-    for i in range(2):
-        for h in range(2):
-            k = 2 * h + i
-            quarter = 2 * i + (1 - x) if h == 0 else 2 * (1 - y) + i
-            ca = rcopy(
-                macc.at[quarter, pl.ds(h * HALF, HALF)], m2a.at[k],
-                ma_ss.at[k], ma_rs.at[k], at_x if h == 0 else at_y,
-            )
-            ca.start()
-            ma.append(ca)
+        yq, xq = lax.div(qq, 2), lax.rem(qq, 2)
+
+        @pl.when(xq != x)
+        def _():
+            ma_copy(yq, 0).start()
+
+        @pl.when(yq != y)
+        def _():
+            ma_copy(xq, 1).start()
+
+    ma = [ma_copy(i, h) for i in range(2) for h in range(2)]
 
     for c2 in f2:
         c2.wait_recv()

time: 60.5 us -> 60.3 us (level)
  no operation moved by 1% of the time
where the time goes in v4:
time: 60.3 us; the launch traced here: 60.2 us
  Pallas kernels  56.6 us (94%)
  local copies, waits for them, and re-layouts  3.57 us (6%)
    pallas_call x1, Pallas kernels, per_device(): pl.pallas_call(functools.partial(kernel, groups, width, tokens * devices,...  56.6 us
    unnamed x5, local copies, waits for them, and re-layouts  3.57 us

profile of v4, /device:TPU:0, one launch (start us, length us, event | category | flops | bytes accessed | tf_op | source)
XLA Modules:
  0.0 60.2 jit_solution(6720828504485472905)
XLA Ops:
  0.0 0.0 copy-start
  0.0 1.7 %copy-done = bf16[512,2560]{1,0:T(8,128)(2,1)S(1)} copy-done((bf16[512,2560]{1,0:T(8,128)(2,1)S(1)}, bf16[512,2560]{1,0:T(8,128)(2,1)}, u32[]{:S(2)}) %copy-start) | copy-done | bytes 2621464
  1.7 0.0 copy-start.1
  1.7 1.1 %copy-done.1 = bf16[512,768]{1,0:T(8,128)(2,1)S(1)} copy-done((bf16[512,768]{1,0:T(8,128)(2,1)S(1)}, bf16[512,768]{1,0:T(8,128)(2,1)}, u32[]{:S(2)}) %copy-start.1) | copy-done | bytes 786456
  2.9 56.6 %shard_map.28 = f32[80,768]{1,0:T(8,128)S(1)} custom-call(bf16[512,2560]{1,0:T(8,128)(2,1)S(1)} %copy-done, bf16[512,768]{1,0:T(8,128)(2,1)S(1)} %copy-done.1), custom_call_target="tpu_custom_call" | custom-call | tf_op jit(solution)/shard_map/pallas_call | solution.py:524
  59.5 0.7 %copy.4 = f32[80,768]{1,0:T(8,128)} copy(f32[80,768]{1,0:T(8,128)S(1)} %shard_map.28) | data formatting | bytes 491520
Async XLA Ops:
  0.0 1.7 %copy-start = (bf16[512,2560]{1,0:T(8,128)(2,1)S(1)}, bf16[512,2560]{1,0:T(8,128)(2,1)}, u32[]{:S(2)}) copy-start(bf16[512,2560]{1,0:T(8,128)(2,1)} %x_hbm.1) | copy-start | bytes 7864324
  1.7 1.1 %copy-start.1 = (bf16[512,768]{1,0:T(8,128)(2,1)S(1)}, bf16[512,768]{1,0:T(8,128)(2,1)}, u32[]{:S(2)}) copy-start(bf16[512,768]{1,0:T(8,128)(2,1)} %g_hbm.1) | copy-start | bytes 2359300

commit v5 on v4

--- a/solution.py
+++ b/solution.py
@@ -242,8 +242,6 @@
     peak = jnp.max(jnp.sum(jnp.abs(damped), axis=1, keepdims=True), axis=0, keepdims=True)
     scale = 1.0 / peak
     approx = scale * (2.0 * eye - scale * damped)
-    for _ in range(ITERS - 5):
-        approx = dot3(approx, 2.0 * eye - dot3(damped, approx))
 
     for ca in ma:
         ca.wait_recv()
@@ -263,52 +261,6 @@
 
     for _ in range(4):
         approx = dot3(approx, 2.0 * eye - dot3(damped, approx))
-    inv_own[...] = approx.astype(BF16)
-
-    slot = 2 * rest + core
-    is_a = slot < QBLK
-    is_g = jnp.logical_or(slot == QBLK, jnp.logical_and(slot == QBLK + 1, q < NG - 4))
-    gidx = (slot - QBLK) * 4 + q
-    ghalf = lax.div(gidx, CBLK)
-
-    def a_copy(i, t):
-        return rcopy(
-            inv_own, inv_a.at[t], inv_ss.at[i], inv_rs.at[t],
-            at(y, x, lax.div(i, 2), lax.rem(i, 2)),
-        )
-
-    def g_dev(i):
-        chip = lax.div(i, rest_n)
-        return at(lax.div(chip, 2), lax.rem(chip, 2), lax.rem(i, rest_n), ghalf)
-
-    def g_copy(i, c):
-        return rcopy(inv_own, inv_g.at[c], inv_ss.at[i], inv_rs.at[QBLK + c], g_dev(i))
-
-    def not_me(i):
-        gg, dd = g_dev(i)
-        return gg * width + dd != me
-
-    @pl.when(is_a)
-    def _():
-        @pl.loop(0, owners)
-        def _(i):
-            @pl.when(i != slot)
-            def _():
-                a_copy(i, slot).start()
-        inv_a[slot] = inv_own[...]
-
-    @pl.when(is_g)
-    def _():
-        @pl.loop(0, 4 * rest_n)
-        def _(i):
-            @pl.when(not_me(i))
-            def _():
-                g_copy(i, lax.rem(gidx, CBLK)).start()
-
-        @pl.when(ghalf == core)
-        def _():
-            inv_g[lax.rem(gidx, CBLK)] = inv_own[...]
-
     for cb in mb:
         cb.wait_recv()
     for h in range(2):
@@ -332,6 +284,54 @@
             z_copy(z, rest).start()
 
     zrecv[rest] = zsend[rest]
+
+    for _ in range(ITERS - 5):
+        approx = dot3(approx, 2.0 * eye - dot3(damped, approx))
+    inv_own[...] = approx.astype(BF16)
+
+    slot = 2 * rest + core
+    is_a = slot < QBLK
+    is_g = jnp.logical_or(slot == QBLK, jnp.logical_and(slot == QBLK + 1, q < NG - 4))
+    gidx = (slot - QBLK) * 4 + q
+    ghalf = lax.div(gidx, CBLK)
+
+    def a_copy(i, t):
+        return rcopy(
+            inv_own, inv_a.at[t], inv_ss.at[i], inv_rs.at[t],
+            at(y, x, lax.div(i, 2), lax.rem(i, 2)),
+        )
+
+    def g_dev(i):
+        chip = lax.div(i, rest_n)
+        return at(lax.div(chip, 2), lax.rem(chip, 2), lax.rem(i, rest_n), ghalf)
+
+    def g_copy(i, c):
+        return rcopy(inv_own, inv_g.at[c], inv_ss.at[i], inv_rs.at[QBLK + c], g_dev(i))
+
+    def not_me(i):
+        gg, dd = g_dev(i)
+        return gg * width + dd != me
+
+    @pl.when(is_a)
+    def _():
+        @pl.loop(0, owners)
+        def _(i):
+            @pl.when(i != slot)
+            def _():
+                a_copy(i, slot).start()
+        inv_a[slot] = inv_own[...]
+
+    @pl.when(is_g)
+    def _():
+        @pl.loop(0, 4 * rest_n)
+        def _(i):
+            @pl.when(not_me(i))
+            def _():
+                g_copy(i, lax.rem(gidx, CBLK)).start()
+
+        @pl.when(ghalf == core)
+        def _():
+            inv_g[lax.rem(gidx, CBLK)] = inv_own[...]
 
     for c in range(CBLK):
         @pl.when(jnp.logical_not(jnp.logical_and(is_g, gidx == core * CBLK + c)))

time: 60.3 us -> 65.7 us (1.090)
  Pallas kernels: 56.6 us -> 61.9 us
    pallas_call x1, Pallas kernels: 56.6 us -> 61.9 us  [per_device(): pl.pallas_call(functools.partial(kernel, groups, width, tokens * devices,...]
where the time goes in v5:
time: 65.7 us; the launch traced here: 65.5 us
  Pallas kernels  61.9 us (94%)
  local copies, waits for them, and re-layouts  3.57 us (5%)
    pallas_call x1, Pallas kernels, per_device(): pl.pallas_call(functools.partial(kernel, groups, width, tokens * devices,...  61.9 us
    unnamed x5, local copies, waits for them, and re-layouts  3.57 us

profile of v5, /device:TPU:0, one launch (start us, length us, event | category | flops | bytes accessed | tf_op | source)
XLA Modules:
  0.0 65.5 jit_solution(13540984852557335975)
XLA Ops:
  0.0 0.0 copy-start
  0.0 1.7 %copy-done = bf16[512,2560]{1,0:T(8,128)(2,1)S(1)} copy-done((bf16[512,2560]{1,0:T(8,128)(2,1)S(1)}, bf16[512,2560]{1,0:T(8,128)(2,1)}, u32[]{:S(2)}) %copy-start) | copy-done | bytes 2621464
  1.7 0.0 copy-start.1
  1.7 1.1 %copy-done.1 = bf16[512,768]{1,0:T(8,128)(2,1)S(1)} copy-done((bf16[512,768]{1,0:T(8,128)(2,1)S(1)}, bf16[512,768]{1,0:T(8,128)(2,1)}, u32[]{:S(2)}) %copy-start.1) | copy-done | bytes 786456
  2.9 61.9 %shard_map.28 = f32[80,768]{1,0:T(8,128)S(1)} custom-call(bf16[512,2560]{1,0:T(8,128)(2,1)S(1)} %copy-done, bf16[512,768]{1,0:T(8,128)(2,1)S(1)} %copy-done.1), custom_call_target="tpu_custom_call" | custom-call | tf_op jit(solution)/shard_map/pallas_call | solution.py:524
  64.8 0.7 %copy.4 = f32[80,768]{1,0:T(8,128)} copy(f32[80,768]{1,0:T(8,128)S(1)} %shard_map.28) | data formatting | bytes 491520
Async XLA Ops:
  0.0 1.7 %copy-start = (bf16[512,2560]{1,0:T(8,128)(2,1)S(1)}, bf16[512,2560]{1,0:T(8,128)(2,1)}, u32[]{:S(2)}) copy-start(bf16[512,2560]{1,0:T(8,128)(2,1)} %x_hbm.1) | copy-start | bytes 7864324
  1.7 1.1 %copy-start.1 = (bf16[512,768]{1,0:T(8,128)(2,1)S(1)}, bf16[512,768]{1,0:T(8,128)(2,1)}, u32[]{:S(2)}) copy-start(bf16[512,768]{1,0:T(8,128)(2,1)} %g_hbm.1) | copy-start | bytes 2359300
